TPU v7x, 256 devices: a whole 4x4x8 slice. The times are simulated.
256 devices in a mesh: group: 32 (over y, x, core), tensor: 8 (over z).
Axes of the slice: x: 4, y: 4, z: 8, core: 2. Of those that a mesh axis runs over, the one named last changes fastest.
Arguments:
- hidden: bfloat16 [32, 2, 256, 4096], P('group', None, 'tensor'), may hold values from -6 to 6
- norm_gain: bfloat16 [4096], replicated, may hold values from 0.5 to 1.5
- w_query: bfloat16 [4096, 4096], P(None, 'tensor'), may hold values from -0.09375 to 0.09375
- w_key: bfloat16 [4096, 1024], P(None, 'tensor'), may hold values from -0.09375 to 0.09375
- w_value: bfloat16 [4096, 1024], P(None, 'tensor'), may hold values from -0.09375 to 0.09375
- w_output: bfloat16 [4096, 4096], P('tensor'), may hold values from -0.09375 to 0.09375
- prefix_pool: bfloat16 [65536, 8, 2048], P('group', None, 'tensor'), may hold values from -120 to 120
- page_table: int32 [32, 2, 1024], P('group'), may hold values from 0 to 1023, each once within a row
- prefix_len: int32 [32, 2], replicated, may hold values from 1024 to 8192
- source: int32 [32], replicated, may hold values from 0 to 31, as said below
- decode_owner: int32 [32, 32], replicated, may hold values from 0 to 31, as said below
Outputs:
- layer_out: bfloat16 [8192, 4096], P(('group', 'tensor'))
- decode_pool: bfloat16 [1024, 8, 2048], P('group', None, 'tensor')
Inputs may be any that keep to these rules, and one draw needn't show every extreme that they name: source[h] is h or h - 1 modulo 32. For each page index k, the values decode_owner[h, k] over all h are all different; no row names one group more than 2 times, and some row names a group exactly 2 times.
All inputs are finite; a program needn't handle non-finite values.
Results may differ from a plain program's by a relative error of at most 0.012.
Values may be sent and summed in bfloat16 or wider, within the bound.
No kernel may reach another device: no remote copies, remote signals or barrier semaphores. Data moves between devices by JAX's collectives and lax.ppermute only.
A program may use at most 128 MiB of HBM per device.

v0:
```python
import functools
import math

import jax
import jax.numpy as jnp
from jax import lax
from jax.experimental import pallas as pl
from jax.experimental.pallas import tpu as pltpu
from jax.sharding import PartitionSpec as P

HD = 128
PAGE = 8
BLOCK = 256
PREFIX = 8192
EPS = 1e-05
THETA = 500000.0

NT = 8
HEADS = 4
SHARD = BLOCK // NT
TILE = 256
KBLK = 512
KEYS = PREFIX + BLOCK
NCH = 4
CHROWS = PREFIX // NCH
COPIES = 8
SLOTS = 2
NEW_KEYS = slice(HEADS * BLOCK, (HEADS + 1) * BLOCK)
NEW_VALUES = slice((HEADS + 1) * BLOCK, (HEADS + 2) * BLOCK)
MASKED = -1e30
EXP_SCALE = math.log2(math.e) / math.sqrt(HD)
MIB = 1 << 20
F32 = jnp.float32
BF16 = jnp.bfloat16

VMEM = pl.BlockSpec(memory_space=pltpu.VMEM)
SMEM = pl.BlockSpec(memory_space=pltpu.SMEM)
ANY = pl.BlockSpec(memory_space=pl.ANY)
HBM = pl.BlockSpec(memory_space=pltpu.HBM)


def shift(value, axis, distance):
    count = lax.axis_size(axis)
    return lax.ppermute(value, axis, [(i, (i + distance) % count) for i in range(count)])


def norm_kernel(take_ref, own_ref, handed_ref, gain_ref, slot_ref, *refs):
    rows_ref, normed_ref, _ = refs[-3:]
    take = take_ref[0] != 0
    rows = jnp.where(take, handed_ref[...].astype(F32), own_ref[...].astype(F32))
    rows_ref[...] = rows.astype(BF16)
    mean_square = jnp.mean(rows * rows, axis=-1, keepdims=True)
    normed_ref[...] = (rows * lax.rsqrt(mean_square + EPS) * gain_ref[...].astype(F32)).astype(BF16)


def choose_and_norm(take, own, handed, gain, slot, *before):
    return pl.pallas_call(
        norm_kernel,
        out_shape=[jax.ShapeDtypeStruct(own.shape, BF16)] * 2 + [jax.ShapeDtypeStruct(slot.shape, BF16)],
        in_specs=[SMEM, VMEM, VMEM, VMEM, HBM] + [ANY] * len(before),
        out_specs=[VMEM, VMEM, HBM],
        input_output_aliases={4: 2},
        compiler_params=pltpu.CompilerParams(vmem_limit_bytes=8 * MIB),
        cost_estimate=pl.CostEstimate(flops=10**6, bytes_accessed=10**6, transcendentals=0),
        name="choose_and_norm",
    )(take, own, handed, gain, slot, *before)


def later_kernel(count, *refs):
    for source_ref, out_ref in zip(refs[:count], refs[-count:]):
        out_ref[...] = source_ref[...]


def later(arrays, *before):
    return pl.pallas_call(
        functools.partial(later_kernel, len(arrays)),
        out_shape=[jax.ShapeDtypeStruct(x.shape, x.dtype) for x in arrays],
        in_specs=[VMEM] * len(arrays) + [ANY] * len(before),
        out_specs=[VMEM] * len(arrays),
        compiler_params=pltpu.CompilerParams(vmem_limit_bytes=4 * MIB),
        cost_estimate=pl.CostEstimate(flops=0, bytes_accessed=10**4, transcendentals=0),
        name="later",
    )(*arrays, *before)


def part_kernel(start, pool_hbm, *refs):
    out_hbm, stage_ref, in_sems, out_sems = refs[-4:]
    size = out_hbm.shape[0] // COPIES
    loads, stores = [], []
    for n in range(COPIES):
        part = pl.ds(n * size, size)
        source = pool_hbm.at[pl.ds(start + n * size, size)]
        loads.append(pltpu.make_async_copy(source, stage_ref.at[part], in_sems.at[n]))
        stores.append(pltpu.make_async_copy(stage_ref.at[part], out_hbm.at[part], out_sems.at[n]))
    for load in loads:
        load.start()
    for load, store in zip(loads, stores):
        load.wait()
        store.start()
    for store in stores:
        store.wait()


def second_slot(pool, *after):
    start = pool.shape[0] // 2
    shape = (start,) + pool.shape[1:]
    return pl.pallas_call(
        functools.partial(part_kernel, start),
        out_shape=jax.ShapeDtypeStruct(shape, BF16),
        in_specs=[HBM] + [ANY] * len(after),
        out_specs=HBM,
        scratch_shapes=[
            pltpu.VMEM(shape, BF16),
            pltpu.SemaphoreType.DMA((COPIES,)),
            pltpu.SemaphoreType.DMA((COPIES,)),
        ],
        compiler_params=pltpu.CompilerParams(vmem_limit_bytes=58 * MIB),
        cost_estimate=pl.CostEstimate(flops=0, bytes_accessed=9 * 10**6, transcendentals=0),
        name="second_slot",
    )(pool, *after)


def qkv_kernel(z_ref, slot_ref, *refs):
    shards = refs[:NT]
    cos_ref, sin_ref, wq_hbm, wk_hbm, wv_hbm, _, q_ref, send_ref = refs[NT : NT + 8]
    x_ref, wq_ref, wk_ref, wv_ref, shard_sem, sems = refs[NT + 8 :]
    z = z_ref[0]
    gathers = []
    for relative, shard in enumerate(shards):
        place = lax.rem(z + relative, NT)
        to = x_ref.at[pl.ds(pl.multiple_of(place * SHARD, SHARD), SHARD)]
        gathers.append(pltpu.make_async_copy(shard, to, shard_sem.at[relative]))
    copies = [
        pltpu.make_async_copy(src, dst, sems.at[n])
        for n, (src, dst) in enumerate([(wk_hbm, wk_ref), (wv_hbm, wv_ref)])
    ]
    half = wq_hbm.shape[0] // 2
    copies += [
        pltpu.make_async_copy(wq_hbm.at[pl.ds(n * half, half)], wq_ref.at[pl.ds(n * half, half)], sems.at[2 + n])
        for n in range(2)
    ]
    for copy in gathers + copies:
        copy.start()
    cosine = cos_ref[...]
    sine = sin_ref[...]

    def rotated(values):
        return values * cosine + pltpu.roll(values, HD // 2, 1) * sine

    for copy in gathers:
        copy.wait()
    copies[0].wait()
    new_keys = rotated(jnp.dot(x_ref[...], wk_ref[...], preferred_element_type=F32))
    q_ref[NEW_KEYS] = new_keys.astype(BF16)
    copies[1].wait()
    new_values = jnp.dot(x_ref[...], wv_ref[...], preferred_element_type=F32)
    q_ref[NEW_VALUES] = new_values.astype(BF16)
    for k in range(BLOCK // PAGE):
        slot = slot_ref[k]
        send_ref[slot, :, :HD] = new_keys[k * PAGE : (k + 1) * PAGE].astype(BF16)
        send_ref[slot, :, HD:] = new_values[k * PAGE : (k + 1) * PAGE].astype(BF16)
    copies[2].wait()
    copies[3].wait()
    for pair in range(HEADS // 2):
        both = jnp.dot(x_ref[...], wq_ref[:, pair * 2 * HD : (pair + 1) * 2 * HD], preferred_element_type=F32)
        for one in range(2):
            head = rotated(both[:, one * HD : (one + 1) * HD]).astype(BF16)
            n = pair * 2 + one
            for shard in range(NT):
                at = (shard * HEADS + n) * SHARD
                q_ref[at : at + SHARD] = head[shard * SHARD : (shard + 1) * SHARD]


def project(z, slots, count, shards, cosine, sine, w_query, w_key, w_value, bias):
    depth, query_width = w_query.shape
    return pl.pallas_call(
        qkv_kernel,
        out_shape=[
            jax.ShapeDtypeStruct(((HEADS + 2) * BLOCK, HD), BF16),
            jax.ShapeDtypeStruct((count, PAGE, 2 * HD), BF16),
        ],
        in_specs=[SMEM, SMEM] + [HBM] * NT + [VMEM] * 2 + [HBM] * 3 + [ANY],
        out_specs=[VMEM, VMEM],
        scratch_shapes=[
            pltpu.VMEM((BLOCK, depth), BF16),
            pltpu.VMEM(w_query.shape, BF16),
            pltpu.VMEM(w_key.shape, BF16),
            pltpu.VMEM(w_value.shape, BF16),
            pltpu.SemaphoreType.DMA((NT,)),
            pltpu.SemaphoreType.DMA((4,)),
        ],
        compiler_params=pltpu.CompilerParams(vmem_limit_bytes=58 * MIB),
        cost_estimate=pl.CostEstimate(
            flops=2 * BLOCK * depth * (query_width + 2 * HD), bytes_accessed=9 * 10**6, transcendentals=0
        ),
        name="project",
    )(z, slots, *shards, cosine, sine, w_query, w_key, w_value, bias)


def attention_kernel(picks, load, split, passed, info_ref, q_ref, bias_ref, *refs):
    if load:
        wo_hbm, pool_hbm, handed_hbm, *refs = refs
        kv_ref, att_ref, wo_ref, wo_sem, kv_sem = refs[-5:]
        out_refs = refs[passed : -5]
    else:
        wo_hbm, kv_ref, *refs = refs
        *out_refs, att_ref, wo_ref, wo_sem = refs[passed:]
    z = info_ref[0]
    take = info_ref[1]

    def cache_copy(n, source):
        part = pl.ds(pl.multiple_of(n * CHROWS, CHROWS), CHROWS)
        return pltpu.make_async_copy(source.at[part], kv_ref.at[part], kv_sem.at[n])

    if load:

        @pl.when(take != 0)
        def _():
            for n in range(NCH):
                cache_copy(n, handed_hbm).start()

        @pl.when(take == 0)
        def _():
            for n in range(NCH):
                cache_copy(n, pool_hbm).start()

    wo_copy = pltpu.make_async_copy(wo_hbm, wo_ref, wo_sem)
    wo_copy.start()
    places = [lax.rem(z + pick, NT) for pick in picks]
    rows = HEADS * SHARD
    queries = jnp.concatenate([q_ref[pl.ds(pl.multiple_of(place * rows, rows), rows)] for place in places], axis=0)

    def scores(keys):
        return lax.dot_general(queries, keys, (((1,), (1,)), ((), ())), preferred_element_type=F32)

    def new_scores():
        block = scores(q_ref[NEW_KEYS])
        place = lax.broadcasted_iota(jnp.int32, (TILE, BLOCK), 0)
        row = place % SHARD + SHARD * jnp.where(place < TILE // 2, places[0], places[1])
        column = lax.broadcasted_iota(jnp.int32, (TILE, BLOCK), 1)
        return jnp.where(column <= row, block, MASKED)

    def stored_scores(at):
        at = pl.multiple_of(at, KBLK)
        return scores(kv_ref[pl.ds(at, KBLK), :HD]) + bias_ref[:, pl.ds(at, KBLK)]

    def fold(block, values, row_max, total, sums):
        lanes = [slice(c * HD, (c + 1) * HD) for c in range(block.shape[1] // HD)]
        top = block[:, lanes[0]]
        for lane in lanes[1:]:
            top = jnp.maximum(top, block[:, lane])
        raised = jnp.maximum(row_max, jnp.max(top, axis=1, keepdims=True))
        keep = jnp.exp2((row_max - raised) * EXP_SCALE)
        e = jnp.exp2((block - raised) * EXP_SCALE)
        total = total * keep
        for lane in lanes:
            total = total + e[:, lane]
        return raised, total, sums * keep + jnp.dot(e.astype(BF16), values, preferred_element_type=F32)

    def chunk(c, carry):
        base = pl.multiple_of(c * CHROWS, CHROWS)
        if load:
            cache_copy(c, pool_hbm).wait()
        block = stored_scores(base)
        for n in range(CHROWS // KBLK):
            following = stored_scores(base + (n + 1) * KBLK) if (n + 1) * KBLK < CHROWS else None
            values = kv_ref[pl.ds(pl.multiple_of(base + n * KBLK, KBLK), KBLK), HD:]
            carry = fold(block, values, *carry)
            block = following
        return carry

    zeros = jnp.zeros((TILE, HD), F32)
    carry = fold(new_scores(), q_ref[NEW_VALUES], jnp.full((TILE, 1), MASKED, F32), zeros, zeros)
    _, total, sums = lax.fori_loop(0, NCH, chunk, carry)
    attended = (sums / jnp.sum(total, axis=1, keepdims=True)).astype(BF16)
    for half in range(2):
        for n in range(HEADS):
            at = half * HEADS * SHARD + n * SHARD
            to = half * SHARD
            att_ref[to : to + SHARD, n * HD : (n + 1) * HD] = attended[at : at + SHARD, :]
    wo_copy.wait()
    product = jnp.dot(att_ref[...], wo_ref[...], preferred_element_type=F32).astype(BF16)
    if split:
        columns = product.shape[1] // 2
        out_refs[0][...] = product[:SHARD, :columns]
        out_refs[1][...] = product[:SHARD, columns:]
        out_refs[2][...] = product[SHARD:]
    else:
        out_refs[0][...] = product[:SHARD]
        out_refs[1][...] = product[SHARD:]


def attend(info, picks, projected, bias, w_output, *held, split=False, after=()):
    load = len(held) == 2
    width = w_output.shape[1]
    part = lambda columns: jax.ShapeDtypeStruct((SHARD, columns), BF16)
    out_shape = [part(width // 2), part(width // 2), part(width)] if split else [part(width)] * 2
    scratch = [pltpu.VMEM((2 * SHARD, HEADS * HD), BF16), pltpu.VMEM(w_output.shape, BF16), pltpu.SemaphoreType.DMA]
    if load:
        scratch += [pltpu.SemaphoreType.DMA((NCH,))]
    extra = [jax.ShapeDtypeStruct((PREFIX, 2 * HD), BF16)] if load else []
    return pl.pallas_call(
        functools.partial(attention_kernel, picks, load, split, len(after)),
        out_shape=out_shape + extra,
        in_specs=[SMEM, VMEM, VMEM, HBM] + ([HBM, HBM] if load else [VMEM]) + [ANY] * len(after),
        out_specs=[VMEM] * len(out_shape + extra),
        scratch_shapes=scratch,
        compiler_params=pltpu.CompilerParams(vmem_limit_bytes=(46 if load else 24) * MIB),
        cost_estimate=pl.CostEstimate(
            flops=8 * TILE * KEYS * HD, bytes_accessed=9 * 10**6, transcendentals=TILE * KEYS
        ),
        name="attend",
    )(info, projected, bias, w_output, *held, *after)


def plus(a, b):
    return a.astype(F32) + b.astype(F32)


def widen_kernel(up_ref, down_ref, from_left_ref, from_right_ref, up_out, down_out):
    half = from_left_ref.shape[1]
    up_out[:, :half] = plus(up_ref[:, :half], from_left_ref[...]).astype(BF16)
    up_out[:, half:] = up_ref[:, half:]
    down_out[:, :half] = down_ref[:, :half]
    down_out[:, half:] = plus(down_ref[:, half:], from_right_ref[...]).astype(BF16)


def add_kernel(up_ref, down_ref, from_left_ref, from_right_ref, up_out, down_out):
    up_out[...] = plus(up_ref[...], from_left_ref[...]).astype(BF16)
    down_out[...] = plus(down_ref[...], from_right_ref[...]).astype(BF16)


def last_kernel(rows_ref, part_ref, from_left_ref, from_right_ref, out_ref):
    branch = part_ref[...].astype(F32) + plus(from_left_ref[...], from_right_ref[...])
    out_ref[...] = (rows_ref[...].astype(F32) + branch).astype(BF16)


def combine(kernel, outputs, name, *arrays):
    shape = jax.ShapeDtypeStruct(arrays[0].shape, BF16)
    return pl.pallas_call(
        kernel,
        out_shape=[shape] * outputs,
        in_specs=[VMEM] * len(arrays),
        out_specs=[VMEM] * outputs,
        compiler_params=pltpu.CompilerParams(vmem_limit_bytes=8 * MIB),
        cost_estimate=pl.CostEstimate(flops=10**6, bytes_accessed=2 * 10**6, transcendentals=0),
        name=name,
    )(*arrays)


def pick_kernel(source_ref, pages_ref, out_ref):
    for k in range(out_ref.shape[0]):
        out_ref[k] = pages_ref[source_ref[k]]


def pick_pages(sources, pages, count):
    return pl.pallas_call(
        pick_kernel,
        out_shape=jax.ShapeDtypeStruct((count,) + pages.shape[1:], BF16),
        in_specs=[SMEM, VMEM],
        out_specs=VMEM,
        compiler_params=pltpu.CompilerParams(vmem_limit_bytes=4 * MIB),
        cost_estimate=pl.CostEstimate(flops=0, bytes_accessed=4 * 10**5, transcendentals=0),
        name="pick_pages",
    )(sources, pages)


def local(
    hidden,
    norm_gain,
    w_query,
    w_key,
    w_value,
    w_output,
    prefix_pool,
    page_table,
    prefix_len,
    source,
    decode_owner,
):
    groups = lax.axis_size("group")
    group = lax.axis_index("group")
    z = lax.axis_index("tensor")
    lower = (group + groups - 1) % groups
    take = source[group] == lower
    take_flag = take.astype(jnp.int32)

    sent_rows = hidden[0, 1]
    sent_table = page_table[0, 1]
    handed_rows = shift(sent_rows, "group", 1)
    handed_table = shift(sent_table, "group", 1)
    pages = prefix_pool.shape[0] // 2
    slot = second_slot(prefix_pool, sent_rows, sent_table)
    rows, normed, slot = choose_and_norm(
        take_flag[None], hidden[0, 0], handed_rows, norm_gain[None], slot, handed_table[None]
    )
    handed = shift(slot, "group", 1).reshape(PREFIX, 2 * HD)

    up, down = [normed], [normed]
    for _ in range(NT // 2 - 1):
        up.append(shift(up[-1], "tensor", 1))
        down.append(shift(down[-1], "tensor", -1))
    prefix_len, decode_owner, handed_table = later((prefix_len, decode_owner, handed_table[None]), up[1])
    count = jnp.where(take, prefix_len[lower, 1], prefix_len[group, 0])
    half = SHARD // 2
    opposite = jnp.concatenate([shift(up[-1][:half], "tensor", 1), shift(down[-1][half:], "tensor", -1)], axis=0)
    shards = down + [opposite] + up[:0:-1]

    table = jnp.where(take, handed_table[0], page_table[0, 0])
    order = jnp.arange(pages, dtype=jnp.int32)
    place = jnp.sum(jnp.where(table[:, None] == order[None, :], order[:, None], 0), axis=0)
    position = place[:, None] * PAGE + jnp.arange(PAGE, dtype=jnp.int32)[None, :]
    bias = jnp.where(position < count, 0.0, MASKED).astype(F32).reshape(1, PREFIX)

    positions = (count + jnp.arange(BLOCK, dtype=jnp.int32)).astype(F32)
    frequency = THETA ** (-(jnp.arange(HD // 2, dtype=F32) * 2.0) / HD)
    angles = positions[:, None] * frequency
    cosine = jnp.cos(angles)
    sine = jnp.sin(angles)
    cosine = jnp.concatenate([cosine, cosine], axis=1)
    sine = jnp.concatenate([-sine, sine], axis=1)

    page_count = BLOCK // PAGE
    ids = jnp.arange(page_count, dtype=jnp.int32)
    same = jnp.logical_and(decode_owner[:, :, None] == decode_owner[:, None, :], ids[None, None, :] < ids[None, :, None])
    ranks = jnp.sum(same.astype(jnp.int32), axis=-1)
    slots = decode_owner[group] * SLOTS + ranks[group]
    mine = decode_owner == group
    senders = jnp.arange(groups, dtype=jnp.int32)[:, None] * SLOTS + ranks
    sources = jnp.sum(jnp.where(mine, senders, 0), axis=0)
    projected, outgoing = project(
        z[None], slots, groups * SLOTS, shards, cosine, sine, w_query, w_key, w_value, bias
    )
    incoming = lax.all_to_all(outgoing, "group", split_axis=0, concat_axis=0, tiled=True)
    kv_pool = pick_pages(sources, incoming, page_count)

    info = jnp.stack([z.astype(jnp.int32), take_flag])
    pool = prefix_pool.reshape(2 * PREFIX, 2 * HD)

    work = (projected, bias, w_output)
    left, right, own_part, cache = attend(info, (4, 0), *work, pool, handed, split=True)
    ups, downs = {}, {}
    ups[3], downs[3] = attend(info, (3, 5), *work, cache)
    ups[2], downs[2], cache = attend(info, (2, 6), *work, pool, handed, after=(incoming,))
    ups[1], downs[1] = attend(info, (1, 7), *work, cache)
    going_up, going_down = shift(left, "tensor", 1), shift(right, "tensor", -1)
    for distance in (3, 2, 1):
        kernel = widen_kernel if distance == 3 else add_kernel
        going_up, going_down = combine(kernel, 2, "add_parts", ups[distance], downs[distance], going_up, going_down)
        going_up, going_down = shift(going_up, "tensor", 1), shift(going_down, "tensor", -1)
    (layer_out,) = combine(last_kernel, 1, "add_rows", rows, own_part, going_up, going_down)
    return (layer_out, kv_pool)


def solution(mesh):
    return jax.shard_map(
        local,
        mesh=mesh,
        in_specs=(
            P("group", None, "tensor", None),
            P(),
            P(None, "tensor"),
            P(None, "tensor"),
            P(None, "tensor"),
            P("tensor", None),
            P("group", None, "tensor"),
            P("group", None, None),
            P(),
            P(),
            P(),
        ),
        out_specs=(P(("group", "tensor"), None), P("group", None, "tensor")),
        check_vma=False,
    )
```

profile of v0, /device:TPU:0, one launch (start us, length us, event | category | flops | bytes accessed | tf_op | source)
XLA Modules:
  0.0 121.5 jit_solution(6656492449258688804)
XLA Ops:
  0.6 1.1 slice_bitcast_fusion
  1.8 0.8 fusion.5
  2.7 1.3 %dynamic_slice.15 = s32[1]{0:T(128)} dynamic-slice(s32[32]{0:T(128)} %param.20, s32[]{:T(128)S(6)} %select_n.53), dynamic_slice_sizes={1} | dynamic-slice | bytes 12 | tf_op jit(solution)/shard_map/dynamic_slice | solution.py:385
  4.6 0.7 broadcast_in_dim.51.gain_ref
  5.3 3.6 %second_slot.1.slot_ref = bf16[1024,8,256]{2,1,0:T(8,128)(2,1)} custom-call(bf16[2048,8,256]{2,1,0:T(8,128)(2,1)} %pool_hbm.1, bf16[32,4096]{1,0:T(8,128)(2,1)} %copy-done.8, s32[1024]{0:T(1024)} %bitcast.23), custom_call_target="tpu_custom_call" | custom-call | bytes 9000000 | tf_op jit(solution)/shard_map/second_slot/pallas_call | solution.py:107
  9.0 2.0 %collective-permute-done.1 = s32[1024]{0:T(1024)S(1)} collective-permute-done((s32[1024]{0:T(1024)S(1)}, s32[1024]{0:T(1024)S(1)}, u32[]{:S(2)}, u32[]{:S(2)}) %collective-permute-start.1) | collective-permute-done | bytes 4128 | tf_op jit(solution)/shard_map/ppermute | solution.py:44
  11.3 4.2 %collective-permute-start.3 = (bf16[32,4096]{1,0:T(8,128)(2,1)S(1)}, bf16[32,4096]{1,0:T(8,128)(2,1)S(1)}, u32[]{:S(2)}, u32[]{:S(2)}) collective-permute-start(bf16[32,4096]{1,0:T(8,128)(2,1)S(1)} %get-tuple-element.28.refs_0_), channel_id=1, source_target_pairs={{0,7},{1,0},{2,1},{3,2},{4,3},{5,4},{6,5},{7,6},{8,15},{9,8},{10,9... | collective-permute-start | bytes 786440 | tf_op jit(solution)/shard_map/ppermute | solution.py:44
  15.7 10.1 %collective-permute-done.2.refs_3_.refs_7_ = bf16[32,4096]{1,0:T(8,128)(2,1)S(1)} collective-permute-done((bf16[32,4096]{1,0:T(8,128)(2,1)S(1)}, bf16[32,4096]{1,0:T(8,128)(2,1)S(1)}, u32[]{:S(2)}, u32[]{:S(2)}) %collective-permute-start.2) | collective-permute-done | bytes 262176 | tf_op jit(solution)/shard_map/ppermute | solution.py:44
  27.9 3.2 %collective-permute-start.4 = (bf16[32,4096]{1,0:T(8,128)(2,1)S(1)}, bf16[32,4096]{1,0:T(8,128)(2,1)S(1)}, u32[]{:S(2)}, u32[]{:S(2)}) collective-permute-start(bf16[32,4096]{1,0:T(8,128)(2,1)S(1)} %collective-permute-done.3.refs_1_), channel_id=1, source_target_pairs={{0,7},{1,0},{2,1},{3,2},{4,3},{5,4},{6,5},{7,6},{8,15},{9,8},{10,9... | collective-permute-start | bytes 786440 | tf_op jit(solution)/shard_map/ppermute | solution.py:44
  32.2 4.5 %collective-permute-done.4.refs_2_ = bf16[32,4096]{1,0:T(8,128)(2,1)S(1)} collective-permute-done((bf16[32,4096]{1,0:T(8,128)(2,1)S(1)}, bf16[32,4096]{1,0:T(8,128)(2,1)S(1)}, u32[]{:S(2)}, u32[]{:S(2)}) %collective-permute-start.4) | collective-permute-done | bytes 262176 | tf_op jit(solution)/shard_map/ppermute | solution.py:44
  36.6 3.7 %collective-permute-start.5 = (bf16[32,4096]{1,0:T(8,128)(2,1)S(1)}, bf16[32,4096]{1,0:T(8,128)(2,1)S(1)}, u32[]{:S(2)}, u32[]{:S(2)}) collective-permute-start(bf16[32,4096]{1,0:T(8,128)(2,1)S(1)} %collective-permute-done.4.refs_2_), channel_id=1, source_target_pairs={{0,7},{1,0},{2,1},{3,2},{4,3},{5,4},{6,5},{7,6},{8,15},{9,8},{10,9... | collective-permute-start | bytes 786440 | tf_op jit(solution)/shard_map/ppermute | solution.py:44
  40.3 0.8 convert_reduce_fusion
  41.3 3.8 %collective-permute-done.5.refs_3_ = bf16[32,4096]{1,0:T(8,128)(2,1)S(1)} collective-permute-done((bf16[32,4096]{1,0:T(8,128)(2,1)S(1)}, bf16[32,4096]{1,0:T(8,128)(2,1)S(1)}, u32[]{:S(2)}, u32[]{:S(2)}) %collective-permute-start.5) | collective-permute-done | bytes 262176 | tf_op jit(solution)/shard_map/ppermute | solution.py:44
  45.1 3.8 %collective-permute-start.9 = (bf16[16,4096]{1,0:T(8,128)(2,1)S(1)}, bf16[16,4096]{1,0:T(8,128)(2,1)S(1)}, u32[]{:S(2)}, u32[]{:S(2)}) collective-permute-start(bf16[16,4096]{1,0:T(8,128)(2,1)S(1)} %slice.25), channel_id=1, source_target_pairs={{0,7},{1,0},{2,1},{3,2},{4,3},{5,4},{6,5},{7,6},{8,15},{9,8},{10,9... | collective-permute-start | bytes 393224 | tf_op jit(solution)/shard_map/ppermute | solution.py:44
  49.8 0.9 select_n.61.refs_13_.bias_ref
  50.7 0.8 pad_maximum_fusion.1
  51.5 4.0 %collective-permute-done.8 = bf16[16,4096]{1,0:T(8,128)(2,1)} collective-permute-done((bf16[16,4096]{1,0:T(8,128)(2,1)S(1)}, bf16[16,4096]{1,0:T(8,128)(2,1)}, u32[]{:S(2)}, u32[]{:S(2)}) %collective-permute-start.8) | collective-permute-done | bytes 131104 | tf_op jit(solution)/shard_map/ppermute | solution.py:44
  55.5 1.6 %pad_maximum_fusion.refs_4_ = bf16[32,4096]{1,0:T(8,128)(2,1)} fusion(bf16[16,4096]{1,0:T(8,128)(2,1)S(1)} %collective-permute-done.9, bf16[16,4096]{1,0:T(8,128)(2,1)} %collective-permute-done.8), kind=kLoop, calls=%fused_computation.5 | loop fusion | flops 524288 | bytes 524288 | tf_op jit(solution)/shard_map/concatenate | solution.py:406
  57.1 7.5 %project.1 = (bf16[1536,128]{1,0:T(8,128)(2,1)}, bf16[64,8,256]{2,1,0:T(8,128)(2,1)}) custom-call(s32[1]{0:T(128)} %bitcast.6.z_ref, s32[32]{0:T(128)} %fusion.4.slot_ref, bf16[32,4096]{1,0:T(8,128)(2,1)} %copy-done.6, bf16[32,4096]{1,0:T(8,128)(2,1)} %copy-done.11, bf16[32,4096]{1,0:T(8,128)(2,1)} %copy-done.13, bf16[32,4096]{1,0:T(8,128)(2,1)} %copy-done.9, ...), custom_call_target="tpu_custom_call" | custom-call | flops 1610612736 | bytes 9000000 | tf_op jit(solution)/shard_map/project/pallas_call | solution.py:176
  64.6 6.6 %all-to-all-start = ((bf16[64,8,256]{2,1,0:T(8,128)(2,1)}), bf16[64,8,256]{2,1,0:T(8,128)(2,1)S(1)}, u32[]{:S(2)}, u32[]{:S(2)}) async-start(bf16[64,8,256]{2,1,0:T(8,128)(2,1)} %get-tuple-element.35), calls=%async_computation | async-start | bytes 524288 | tf_op jit(solution)/shard_map/all_to_all | solution.py:434
  71.3 1.0 copy-done.2
  72.3 8.5 %attend.4 = (bf16[32,2048]{1,0:T(8,128)(2,1)S(1)}, bf16[32,2048]{1,0:T(8,128)(2,1)S(1)}, bf16[32,4096]{1,0:T(8,128)(2,1)S(1)}, bf16[8192,256]{1,0:T(8,128)(2,1)S(1)}) custom-call(s32[2]{0:T(128)S(1)} %pad_add_fusion.info_ref, bf16[1536,128]{1,0:T(8,128)(2,1)S(1)} %copy-done.2, f32[1,8192]{1,0:T(1,128)S(1)} %copy-done.4, bf16[512,4096]{1,0:T(8,128)(2,1)} %refs_0_.8, ...), custom_call_target="tpu_custom_call" | custom-call | flops 2214592512 | bytes 9000000 | tf_op jit(solution)/shard_map/attend/pallas_call | solution.py:302
  80.8 3.2 %collective-permute-start.12 = (bf16[32,2048]{1,0:T(8,128)(2,1)S(1)}, bf16[32,2048]{1,0:T(8,128)(2,1)S(1)}, u32[]{:S(2)}, u32[]{:S(2)}) collective-permute-start(bf16[32,2048]{1,0:T(8,128)(2,1)S(1)} %get-tuple-element.45), channel_id=1, source_target_pairs={{0,7},{1,0},{2,1},{3,2},{4,3},{5,4},{6,5},{7,6},{8,15},{9,8},{10,9... | collective-permute-start | bytes 393224 | tf_op jit(solution)/shard_map/ppermute | solution.py:44
  84.0 6.4 %attend.7 = (bf16[32,4096]{1,0:T(8,128)(2,1)S(1)}, bf16[32,4096]{1,0:T(8,128)(2,1)S(1)}) custom-call(s32[2]{0:T(128)S(1)} %pad_add_fusion.info_ref, bf16[1536,128]{1,0:T(8,128)(2,1)S(1)} %copy-done.2, f32[1,8192]{1,0:T(1,128)S(1)} %copy-done.4, bf16[512,4096]{1,0:T(8,128)(2,1)S(1)} %copy-done, bf16[8192,256]{1,0:T(8,128)(2,1)S(1)} %get-tuple-element.41.refs_1_), custom_call_target="tpu_custom_call" | custom-call | flops 2214592512 | bytes 9000000 | tf_op jit(solution)/shard_map/attend/pallas_call | solution.py:302
  90.6 3.2 %collective-permute-start.14 = (bf16[32,4096]{1,0:T(8,128)(2,1)S(1)}, bf16[32,4096]{1,0:T(8,128)(2,1)S(1)}, u32[]{:S(2)}, u32[]{:S(2)}) collective-permute-start(bf16[32,4096]{1,0:T(8,128)(2,1)S(1)} %get-tuple-element.47), channel_id=1, source_target_pairs={{0,7},{1,0},{2,1},{3,2},{4,3},{5,4},{6,5},{7,6},{8,15},{9,8},{10,9... | collective-permute-start | bytes 786440 | tf_op jit(solution)/shard_map/ppermute | solution.py:44
  93.8 8.5 %attend.5 = (bf16[32,4096]{1,0:T(8,128)(2,1)S(1)}, bf16[32,4096]{1,0:T(8,128)(2,1)S(1)}, bf16[8192,256]{1,0:T(8,128)(2,1)S(1)}) custom-call(s32[2]{0:T(128)S(1)} %pad_add_fusion.info_ref, bf16[1536,128]{1,0:T(8,128)(2,1)S(1)} %copy-done.3, f32[1,8192]{1,0:T(1,128)S(1)} %copy-done.4, bf16[512,4096]{1,0:T(8,128)(2,1)} %refs_0_.8, bf16[16384,256]{1,0:T(8,128)(2,1)} %bitcast.21, ...), custom_call_target="tpu_custom_call" | custom-call | flops 2214592512 | bytes 9000000 | tf_op jit(solution)/shard_map/attend/pallas_call | solution.py:302
  102.8 3.2 %collective-permute-start.16 = (bf16[32,4096]{1,0:T(8,128)(2,1)S(1)}, bf16[32,4096]{1,0:T(8,128)(2,1)S(1)}, u32[]{:S(2)}, u32[]{:S(2)}) collective-permute-start(bf16[32,4096]{1,0:T(8,128)(2,1)S(1)} %get-tuple-element.49), channel_id=1, source_target_pairs={{0,7},{1,0},{2,1},{3,2},{4,3},{5,4},{6,5},{7,6},{8,15},{9,8},{10,9... | collective-permute-start | bytes 786440 | tf_op jit(solution)/shard_map/ppermute | solution.py:44
  106.0 6.4 %attend.6 = (bf16[32,4096]{1,0:T(8,128)(2,1)S(1)}, bf16[32,4096]{1,0:T(8,128)(2,1)S(1)}) custom-call(s32[2]{0:T(128)S(1)} %pad_add_fusion.info_ref, bf16[1536,128]{1,0:T(8,128)(2,1)S(1)} %copy-done.3, f32[1,8192]{1,0:T(1,128)S(1)} %copy-done.4, bf16[512,4096]{1,0:T(8,128)(2,1)S(1)} %copy-done.1, bf16[8192,256]{1,0:T(8,128)(2,1)S(1)} %get-tuple-element.36.refs_1_), custom_call_target="tpu_custom_call" | custom-call | flops 2214592512 | bytes 9000000 | tf_op jit(solution)/shard_map/attend/pallas_call | solution.py:302
  112.6 3.2 %collective-permute-start.18 = (bf16[32,4096]{1,0:T(8,128)(2,1)S(1)}, bf16[32,4096]{1,0:T(8,128)(2,1)S(1)}, u32[]{:S(2)}, u32[]{:S(2)}) collective-permute-start(bf16[32,4096]{1,0:T(8,128)(2,1)S(1)} %get-tuple-element.51), channel_id=1, source_target_pairs={{0,7},{1,0},{2,1},{3,2},{4,3},{5,4},{6,5},{7,6},{8,15},{9,8},{10,9... | collective-permute-start | bytes 786440 | tf_op jit(solution)/shard_map/ppermute | solution.py:44
  116.0 1.2 %pick_pages.1 = bf16[32,8,256]{2,1,0:T(8,128)(2,1)} custom-call(s32[32]{0:T(128)S(1)} %select_reduce_fusion.1.source_ref, bf16[64,8,256]{2,1,0:T(8,128)(2,1)S(1)} %all-to-all-done.refs_3_.pages_ref), custom_call_target="tpu_custom_call" | custom-call | bytes 400000 | tf_op jit(solution)/shard_map/pick_pages/pallas_call | solution.py:357
  117.2 3.5 %collective-permute-done.17.from_left_ref = bf16[32,4096]{1,0:T(8,128)(2,1)S(1)} collective-permute-done((bf16[32,4096]{1,0:T(8,128)(2,1)S(1)}, bf16[32,4096]{1,0:T(8,128)(2,1)S(1)}, u32[]{:S(2)}, u32[]{:S(2)}) %collective-permute-start.17) | collective-permute-done | bytes 262176 | tf_op jit(solution)/shard_map/ppermute | solution.py:44
  120.7 0.8 add_rows.1
  (77 shorter events, 4.6 us)
Async XLA Ops:
  1.7 9.2 %collective-permute-start = (bf16[32,4096]{1,0:T(8,128)(2,1)S(1)}, bf16[32,4096]{1,0:T(8,128)(2,1)S(1)}, u32[]{:S(2)}, u32[]{:S(2)}) collective-permute-start(bf16[32,4096]{1,0:T(8,128)(2,1)S(1)} %get-tuple-element.52.refs_0_), channel_id=1, source_target_pairs={{0,8},{8,16},{16,24},{24,32},{32,40},{40,48},{48,56},{56,64},{64,7... | collective-permute-start | bytes 786440 | tf_op jit(solution)/shard_map/ppermute | solution.py:44
  2.6 8.3 %collective-permute-start.1 = (s32[1024]{0:T(1024)S(1)}, s32[1024]{0:T(1024)S(1)}, u32[]{:S(2)}, u32[]{:S(2)}) collective-permute-start(s32[1024]{0:T(1024)S(1)} %bitcast.22), channel_id=1, source_target_pairs={{0,8},{8,16},{16,24},{24,32},{32,40},{40,48},{48,56},{56,64},{64,7... | collective-permute-start | bytes 12296 | tf_op jit(solution)/shard_map/ppermute | solution.py:44
  9.0 16.8 %copy-start.7 = (s32[32,32]{1,0:T(8,128)S(1)}, s32[32,32]{1,0:T(8,128)}, u32[]{:S(2)}) copy-start(s32[32,32]{1,0:T(8,128)} %refs_1_.1) | copy-start | bytes 12292
  11.2 45.9 %copy-start.6 = (bf16[32,4096]{1,0:T(8,128)(2,1)}, bf16[32,4096]{1,0:T(8,128)(2,1)S(1)}, u32[]{:S(2)}) copy-start(bf16[32,4096]{1,0:T(8,128)(2,1)S(1)} %get-tuple-element.28.refs_0_) | copy-start | bytes 786436
  11.2 60.0 %collective-permute-start.10 = (bf16[1024,8,256]{2,1,0:T(8,128)(2,1)}, bf16[1024,8,256]{2,1,0:T(8,128)(2,1)}, u32[]{:S(2)}, u32[]{:S(2)}) collective-permute-start(bf16[1024,8,256]{2,1,0:T(8,128)(2,1)} %get-tuple-element.33), channel_id=1, source_target_pairs={{0,8},{8,16},{16,24},{24,32},{32,40},{40,48},{48,56},{56,64},{64,7... | collective-permute-start | bytes 12582920 | tf_op jit(solution)/shard_map/ppermute | solution.py:44
  11.3 16.6 %collective-permute-start.3 = (bf16[32,4096]{1,0:T(8,128)(2,1)S(1)}, bf16[32,4096]{1,0:T(8,128)(2,1)S(1)}, u32[]{:S(2)}, u32[]{:S(2)}) collective-permute-start(bf16[32,4096]{1,0:T(8,128)(2,1)S(1)} %get-tuple-element.28.refs_0_), channel_id=1, source_target_pairs={{0,7},{1,0},{2,1},{3,2},{4,3},{5,4},{6,5},{7,6},{8,15},{9,8},{10,9... | collective-permute-start | bytes 786440 | tf_op jit(solution)/shard_map/ppermute | solution.py:44
  15.5 10.3 %collective-permute-start.2 = (bf16[32,4096]{1,0:T(8,128)(2,1)S(1)}, bf16[32,4096]{1,0:T(8,128)(2,1)S(1)}, u32[]{:S(2)}, u32[]{:S(2)}) collective-permute-start(bf16[32,4096]{1,0:T(8,128)(2,1)S(1)} %get-tuple-element.28.refs_0_), channel_id=1, source_target_pairs={{0,1},{1,2},{2,3},{3,4},{4,5},{5,6},{6,7},{7,0},{8,9},{9,10},{10,1... | collective-permute-start | bytes 786440 | tf_op jit(solution)/shard_map/ppermute | solution.py:44
  25.8 31.3 %copy-start.5 = (bf16[32,4096]{1,0:T(8,128)(2,1)}, bf16[32,4096]{1,0:T(8,128)(2,1)S(1)}, u32[]{:S(2)}) copy-start(bf16[32,4096]{1,0:T(8,128)(2,1)S(1)} %collective-permute-done.2.refs_3_.refs_7_) | copy-start | bytes 786436
  27.8 12.6 %collective-permute-start.6 = (bf16[32,4096]{1,0:T(8,128)(2,1)S(1)}, bf16[32,4096]{1,0:T(8,128)(2,1)S(1)}, u32[]{:S(2)}, u32[]{:S(2)}) collective-permute-start(bf16[32,4096]{1,0:T(8,128)(2,1)S(1)} %collective-permute-done.2.refs_3_.refs_7_), channel_id=1, source_target_pairs={{0,1},{1,2},{2,3},{3,4},{4,5},{5,6},{6,7},{7,0},{8,9},{9,10},{10,1... | collective-permute-start | bytes 786440 | tf_op jit(solution)/shard_map/ppermute | solution.py:44
  27.9 29.2 %copy-start.11 = (bf16[32,4096]{1,0:T(8,128)(2,1)}, bf16[32,4096]{1,0:T(8,128)(2,1)S(1)}, u32[]{:S(2)}) copy-start(bf16[32,4096]{1,0:T(8,128)(2,1)S(1)} %collective-permute-done.3.refs_1_) | copy-start | bytes 786436
  27.9 8.8 %collective-permute-start.4 = (bf16[32,4096]{1,0:T(8,128)(2,1)S(1)}, bf16[32,4096]{1,0:T(8,128)(2,1)S(1)}, u32[]{:S(2)}, u32[]{:S(2)}) collective-permute-start(bf16[32,4096]{1,0:T(8,128)(2,1)S(1)} %collective-permute-done.3.refs_1_), channel_id=1, source_target_pairs={{0,7},{1,0},{2,1},{3,2},{4,3},{5,4},{6,5},{7,6},{8,15},{9,8},{10,9... | collective-permute-start | bytes 786440 | tf_op jit(solution)/shard_map/ppermute | solution.py:44
  36.6 20.5 %copy-start.13 = (bf16[32,4096]{1,0:T(8,128)(2,1)}, bf16[32,4096]{1,0:T(8,128)(2,1)S(1)}, u32[]{:S(2)}) copy-start(bf16[32,4096]{1,0:T(8,128)(2,1)S(1)} %collective-permute-done.4.refs_2_) | copy-start | bytes 786436
  36.6 8.5 %collective-permute-start.5 = (bf16[32,4096]{1,0:T(8,128)(2,1)S(1)}, bf16[32,4096]{1,0:T(8,128)(2,1)S(1)}, u32[]{:S(2)}, u32[]{:S(2)}) collective-permute-start(bf16[32,4096]{1,0:T(8,128)(2,1)S(1)} %collective-permute-done.4.refs_2_), channel_id=1, source_target_pairs={{0,7},{1,0},{2,1},{3,2},{4,3},{5,4},{6,5},{7,6},{8,15},{9,8},{10,9... | collective-permute-start | bytes 786440 | tf_op jit(solution)/shard_map/ppermute | solution.py:44
  40.3 16.8 %copy-start.12 = (bf16[32,4096]{1,0:T(8,128)(2,1)}, bf16[32,4096]{1,0:T(8,128)(2,1)S(1)}, u32[]{:S(2)}) copy-start(bf16[32,4096]{1,0:T(8,128)(2,1)S(1)} %collective-permute-done.6.refs_6_) | copy-start | bytes 786436
  40.3 8.6 %collective-permute-start.7 = (bf16[32,4096]{1,0:T(8,128)(2,1)S(1)}, bf16[32,4096]{1,0:T(8,128)(2,1)S(1)}, u32[]{:S(2)}, u32[]{:S(2)}) collective-permute-start(bf16[32,4096]{1,0:T(8,128)(2,1)S(1)} %collective-permute-done.6.refs_6_), channel_id=1, source_target_pairs={{0,1},{1,2},{2,3},{3,4},{4,5},{5,6},{6,7},{7,0},{8,9},{9,10},{10,1... | collective-permute-start | bytes 786440 | tf_op jit(solution)/shard_map/ppermute | solution.py:44
  45.1 12.0 %copy-start.9 = (bf16[32,4096]{1,0:T(8,128)(2,1)}, bf16[32,4096]{1,0:T(8,128)(2,1)S(1)}, u32[]{:S(2)}) copy-start(bf16[32,4096]{1,0:T(8,128)(2,1)S(1)} %collective-permute-done.5.refs_3_) | copy-start | bytes 786436
  45.1 6.4 %collective-permute-start.9 = (bf16[16,4096]{1,0:T(8,128)(2,1)S(1)}, bf16[16,4096]{1,0:T(8,128)(2,1)S(1)}, u32[]{:S(2)}, u32[]{:S(2)}) collective-permute-start(bf16[16,4096]{1,0:T(8,128)(2,1)S(1)} %slice.25), channel_id=1, source_target_pairs={{0,7},{1,0},{2,1},{3,2},{4,3},{5,4},{6,5},{7,6},{8,15},{9,8},{10,9... | collective-permute-start | bytes 393224 | tf_op jit(solution)/shard_map/ppermute | solution.py:44
  48.9 8.2 %copy-start.10 = (bf16[32,4096]{1,0:T(8,128)(2,1)}, bf16[32,4096]{1,0:T(8,128)(2,1)S(1)}, u32[]{:S(2)}) copy-start(bf16[32,4096]{1,0:T(8,128)(2,1)S(1)} %collective-permute-done.7.refs_5_) | copy-start | bytes 786436
  48.9 6.5 %collective-permute-start.8 = (bf16[16,4096]{1,0:T(8,128)(2,1)S(1)}, bf16[16,4096]{1,0:T(8,128)(2,1)}, u32[]{:S(2)}, u32[]{:S(2)}) collective-permute-start(bf16[16,4096]{1,0:T(8,128)(2,1)S(1)} %slice.24), channel_id=1, source_target_pairs={{0,1},{1,2},{2,3},{3,4},{4,5},{5,6},{6,7},{7,0},{8,9},{9,10},{10,1... | collective-permute-start | bytes 393224 | tf_op jit(solution)/shard_map/ppermute | solution.py:44
  57.1 14.1 %copy-start.4 = (f32[1,8192]{1,0:T(1,128)S(1)}, f32[1,8192]{1,0:T(1,128)}, u32[]{:S(2)}) copy-start(f32[1,8192]{1,0:T(1,128)} %select_n.61.refs_13_.bias_ref) | copy-start | bytes 98308
  64.6 29.2 %all-to-all-start = ((bf16[64,8,256]{2,1,0:T(8,128)(2,1)}), bf16[64,8,256]{2,1,0:T(8,128)(2,1)S(1)}, u32[]{:S(2)}, u32[]{:S(2)}) async-start(bf16[64,8,256]{2,1,0:T(8,128)(2,1)} %get-tuple-element.35), calls=%async_computation | async-start | bytes 524288 | tf_op jit(solution)/shard_map/all_to_all | solution.py:434
  72.2 11.8 %copy-start = (bf16[512,4096]{1,0:T(8,128)(2,1)S(1)}, bf16[512,4096]{1,0:T(8,128)(2,1)}, u32[]{:S(2)}) copy-start(bf16[512,4096]{1,0:T(8,128)(2,1)} %refs_0_.8) | copy-start | bytes 12582916
  80.7 9.7 %collective-permute-start.11 = (bf16[32,2048]{1,0:T(8,128)(2,1)S(1)}, bf16[32,2048]{1,0:T(8,128)(2,1)S(1)}, u32[]{:S(2)}, u32[]{:S(2)}) collective-permute-start(bf16[32,2048]{1,0:T(8,128)(2,1)S(1)} %get-tuple-element.44), channel_id=1, source_target_pairs={{0,1},{1,2},{2,3},{3,4},{4,5},{5,6},{6,7},{7,0},{8,9},{9,10},{10,1... | collective-permute-start | bytes 393224 | tf_op jit(solution)/shard_map/ppermute | solution.py:44
  80.8 9.6 %collective-permute-start.12 = (bf16[32,2048]{1,0:T(8,128)(2,1)S(1)}, bf16[32,2048]{1,0:T(8,128)(2,1)S(1)}, u32[]{:S(2)}, u32[]{:S(2)}) collective-permute-start(bf16[32,2048]{1,0:T(8,128)(2,1)S(1)} %get-tuple-element.45), channel_id=1, source_target_pairs={{0,7},{1,0},{2,1},{3,2},{4,3},{5,4},{6,5},{7,6},{8,15},{9,8},{10,9... | collective-permute-start | bytes 393224 | tf_op jit(solution)/shard_map/ppermute | solution.py:44
  84.0 9.8 %copy-start.3 = (bf16[1536,128]{1,0:T(8,128)(2,1)S(1)}, bf16[1536,128]{1,0:T(8,128)(2,1)}, u32[]{:S(2)}) copy-start(bf16[1536,128]{1,0:T(8,128)(2,1)} %get-tuple-element.32.q_ref) | copy-start | bytes 1179652
  90.5 11.8 %collective-permute-start.13 = (bf16[32,4096]{1,0:T(8,128)(2,1)S(1)}, bf16[32,4096]{1,0:T(8,128)(2,1)S(1)}, u32[]{:S(2)}, u32[]{:S(2)}) collective-permute-start(bf16[32,4096]{1,0:T(8,128)(2,1)S(1)} %get-tuple-element.46), channel_id=1, source_target_pairs={{0,1},{1,2},{2,3},{3,4},{4,5},{5,6},{6,7},{7,0},{8,9},{9,10},{10,1... | collective-permute-start | bytes 786440 | tf_op jit(solution)/shard_map/ppermute | solution.py:44
  90.6 11.7 %collective-permute-start.14 = (bf16[32,4096]{1,0:T(8,128)(2,1)S(1)}, bf16[32,4096]{1,0:T(8,128)(2,1)S(1)}, u32[]{:S(2)}, u32[]{:S(2)}) collective-permute-start(bf16[32,4096]{1,0:T(8,128)(2,1)S(1)} %get-tuple-element.47), channel_id=1, source_target_pairs={{0,7},{1,0},{2,1},{3,2},{4,3},{5,4},{6,5},{7,6},{8,15},{9,8},{10,9... | collective-permute-start | bytes 786440 | tf_op jit(solution)/shard_map/ppermute | solution.py:44
  93.8 12.2 %copy-start.1 = (bf16[512,4096]{1,0:T(8,128)(2,1)S(1)}, bf16[512,4096]{1,0:T(8,128)(2,1)}, u32[]{:S(2)}) copy-start(bf16[512,4096]{1,0:T(8,128)(2,1)} %refs_0_.8) | copy-start | bytes 12582916
  102.5 9.9 %collective-permute-start.15 = (bf16[32,4096]{1,0:T(8,128)(2,1)S(1)}, bf16[32,4096]{1,0:T(8,128)(2,1)S(1)}, u32[]{:S(2)}, u32[]{:S(2)}) collective-permute-start(bf16[32,4096]{1,0:T(8,128)(2,1)S(1)} %get-tuple-element.48), channel_id=1, source_target_pairs={{0,1},{1,2},{2,3},{3,4},{4,5},{5,6},{6,7},{7,0},{8,9},{9,10},{10,1... | collective-permute-start | bytes 786440 | tf_op jit(solution)/shard_map/ppermute | solution.py:44
  102.8 9.6 %collective-permute-start.16 = (bf16[32,4096]{1,0:T(8,128)(2,1)S(1)}, bf16[32,4096]{1,0:T(8,128)(2,1)S(1)}, u32[]{:S(2)}, u32[]{:S(2)}) collective-permute-start(bf16[32,4096]{1,0:T(8,128)(2,1)S(1)} %get-tuple-element.49), channel_id=1, source_target_pairs={{0,7},{1,0},{2,1},{3,2},{4,3},{5,4},{6,5},{7,6},{8,15},{9,8},{10,9... | collective-permute-start | bytes 786440 | tf_op jit(solution)/shard_map/ppermute | solution.py:44
  112.6 8.1 %collective-permute-start.17 = (bf16[32,4096]{1,0:T(8,128)(2,1)S(1)}, bf16[32,4096]{1,0:T(8,128)(2,1)S(1)}, u32[]{:S(2)}, u32[]{:S(2)}) collective-permute-start(bf16[32,4096]{1,0:T(8,128)(2,1)S(1)} %get-tuple-element.50), channel_id=1, source_target_pairs={{0,1},{1,2},{2,3},{3,4},{4,5},{5,6},{6,7},{7,0},{8,9},{9,10},{10,1... | collective-permute-start | bytes 786440 | tf_op jit(solution)/shard_map/ppermute | solution.py:44
  112.6 8.0 %collective-permute-start.18 = (bf16[32,4096]{1,0:T(8,128)(2,1)S(1)}, bf16[32,4096]{1,0:T(8,128)(2,1)S(1)}, u32[]{:S(2)}, u32[]{:S(2)}) collective-permute-start(bf16[32,4096]{1,0:T(8,128)(2,1)S(1)} %get-tuple-element.51), channel_id=1, source_target_pairs={{0,7},{1,0},{2,1},{3,2},{4,3},{5,4},{6,5},{7,6},{8,15},{9,8},{10,9... | collective-permute-start | bytes 786440 | tf_op jit(solution)/shard_map/ppermute | solution.py:44
  (4 other events, 13.9 us)
where the time goes:
time: 124 us; the launch traced here: 121 us
  Pallas kernels  43.4 us (35%)
  starting transfers between devices  35.5 us (29%)
  waiting for transfers between devices  27.7 us (22%)
  local copies, waits for them, and re-layouts  6.55 us (5%)
  other arithmetic  5.25 us (4%)
  between operations  3.04 us (2%)
    pallas_call x4, Pallas kernels, attend(): pl.pallas_call(functools.partial(attention_kernel, picks, load, split, le...  29.7 us
    ppermute x19, starting transfers between devices, shift(): lax.ppermute(value, axis, [(i, (i + distance) % count) for i in range(cou...  28.9 us
    ppermute x19, waiting for transfers between devices, shift(): lax.ppermute(value, axis, [(i, (i + distance) % count) for i in range(cou...  27.7 us
    pallas_call x1, Pallas kernels, project(): pl.pallas_call(qkv_kernel, out_shape=[jax.ShapeDtypeStruct(((HEADS + 2) *...  7.48 us
    all_to_all x1, starting transfers between devices, local(): lax.all_to_all(outgoing, 'group', split_axis=0, concat_axis=0, tiled=True)  6.59 us
    pallas_call x1, Pallas kernels, second_slot(): pl.pallas_call(functools.partial(part_kernel, start), out_shape=jax.Shape...  3.61 us
  transfers between devices with their start and end apart: 20, of which 6 were waited for; matrix products, arithmetic and copies ran while one was open for 8% of the time, Pallas kernels for 35%

commit v1 on v0

--- a/solution.py
+++ b/solution.py
@@ -271,7 +271,12 @@
 
     zeros = jnp.zeros((TILE, HD), F32)
     carry = fold(new_scores(), q_ref[NEW_VALUES], jnp.full((TILE, 1), MASKED, F32), zeros, zeros)
-    _, total, sums = lax.fori_loop(0, NCH, chunk, carry)
+    if 1 in picks:
+        carry = lax.fori_loop(0, NCH, chunk, carry)
+    else:
+        for c in range(NCH):
+            carry = chunk(c, carry)
+    _, total, sums = carry
     attended = (sums / jnp.sum(total, axis=1, keepdims=True)).astype(BF16)
     for half in range(2):
         for n in range(HEADS):

time: 124 us -> 122 us (0.984)
  Pallas kernels: 43.4 us -> 41.9 us
    pallas_call x4, Pallas kernels: 29.7 us -> 28.2 us  [attend(): pl.pallas_call(functools.partial(attention_kernel, picks, load, split, le...]
  transfers between devices with their start and end apart: 20 -> 20, of which waited for: 6 -> 6; matrix products, arithmetic and copies ran while one was open for 8% -> 8% of each run, Pallas kernels for 35% -> 34%
where the time goes in v1:
time: 122 us; the launch traced here: 120 us
  Pallas kernels  41.9 us (34%)
  starting transfers between devices  35.3 us (29%)
  waiting for transfers between devices  27.7 us (23%)
  local copies, waits for them, and re-layouts  6.55 us (5%)
  other arithmetic  5.25 us (4%)
  between operations  3.04 us (2%)
    ppermute x19, starting transfers between devices, shift(): lax.ppermute(value, axis, [(i, (i + distance) % count) for i in range(cou...  28.7 us
    pallas_call x4, Pallas kernels, attend(): pl.pallas_call(functools.partial(attention_kernel, picks, load, split, le...  28.2 us
    ppermute x19, waiting for transfers between devices, shift(): lax.ppermute(value, axis, [(i, (i + distance) % count) for i in range(cou...  27.7 us
    pallas_call x1, Pallas kernels, project(): pl.pallas_call(qkv_kernel, out_shape=[jax.ShapeDtypeStruct(((HEADS + 2) *...  7.48 us
    all_to_all x1, starting transfers between devices, local(): lax.all_to_all(outgoing, 'group', split_axis=0, concat_axis=0, tiled=True)  6.59 us
    pallas_call x1, Pallas kernels, second_slot(): pl.pallas_call(functools.partial(part_kernel, start), out_shape=jax.Shape...  3.61 us
  transfers between devices with their start and end apart: 20, of which 6 were waited for; matrix products, arithmetic and copies ran while one was open for 8% of the time, Pallas kernels for 34%

profile of v1, /device:TPU:0, one launch (start us, length us, event | category | flops | bytes accessed | tf_op | source)
XLA Modules:
  0.0 119.8 jit_solution(15545774960383269763)
XLA Ops:
  0.6 1.1 slice_bitcast_fusion
  1.8 0.8 fusion.5
  2.7 1.3 %dynamic_slice.15 = s32[1]{0:T(128)} dynamic-slice(s32[32]{0:T(128)} %param.20, s32[]{:T(128)S(6)} %select_n.53), dynamic_slice_sizes={1} | dynamic-slice | bytes 12 | tf_op jit(solution)/shard_map/dynamic_slice | solution.py:390
  4.6 0.7 broadcast_in_dim.51.gain_ref
  5.3 3.6 %second_slot.1.slot_ref = bf16[1024,8,256]{2,1,0:T(8,128)(2,1)} custom-call(bf16[2048,8,256]{2,1,0:T(8,128)(2,1)} %pool_hbm.1, bf16[32,4096]{1,0:T(8,128)(2,1)} %copy-done.8, s32[1024]{0:T(1024)} %bitcast.23), custom_call_target="tpu_custom_call" | custom-call | bytes 9000000 | tf_op jit(solution)/shard_map/second_slot/pallas_call | solution.py:107
  9.0 2.0 %collective-permute-done.1 = s32[1024]{0:T(1024)S(1)} collective-permute-done((s32[1024]{0:T(1024)S(1)}, s32[1024]{0:T(1024)S(1)}, u32[]{:S(2)}, u32[]{:S(2)}) %collective-permute-start.1) | collective-permute-done | bytes 4128 | tf_op jit(solution)/shard_map/ppermute | solution.py:44
  11.3 4.2 %collective-permute-start.3 = (bf16[32,4096]{1,0:T(8,128)(2,1)S(1)}, bf16[32,4096]{1,0:T(8,128)(2,1)S(1)}, u32[]{:S(2)}, u32[]{:S(2)}) collective-permute-start(bf16[32,4096]{1,0:T(8,128)(2,1)S(1)} %get-tuple-element.28.refs_0_), channel_id=1, source_target_pairs={{0,7},{1,0},{2,1},{3,2},{4,3},{5,4},{6,5},{7,6},{8,15},{9,8},{10,9... | collective-permute-start | bytes 786440 | tf_op jit(solution)/shard_map/ppermute | solution.py:44
  15.7 10.1 %collective-permute-done.2.refs_3_.refs_7_ = bf16[32,4096]{1,0:T(8,128)(2,1)S(1)} collective-permute-done((bf16[32,4096]{1,0:T(8,128)(2,1)S(1)}, bf16[32,4096]{1,0:T(8,128)(2,1)S(1)}, u32[]{:S(2)}, u32[]{:S(2)}) %collective-permute-start.2) | collective-permute-done | bytes 262176 | tf_op jit(solution)/shard_map/ppermute | solution.py:44
  27.9 3.2 %collective-permute-start.4 = (bf16[32,4096]{1,0:T(8,128)(2,1)S(1)}, bf16[32,4096]{1,0:T(8,128)(2,1)S(1)}, u32[]{:S(2)}, u32[]{:S(2)}) collective-permute-start(bf16[32,4096]{1,0:T(8,128)(2,1)S(1)} %collective-permute-done.3.refs_1_), channel_id=1, source_target_pairs={{0,7},{1,0},{2,1},{3,2},{4,3},{5,4},{6,5},{7,6},{8,15},{9,8},{10,9... | collective-permute-start | bytes 786440 | tf_op jit(solution)/shard_map/ppermute | solution.py:44
  32.2 4.5 %collective-permute-done.4.refs_2_ = bf16[32,4096]{1,0:T(8,128)(2,1)S(1)} collective-permute-done((bf16[32,4096]{1,0:T(8,128)(2,1)S(1)}, bf16[32,4096]{1,0:T(8,128)(2,1)S(1)}, u32[]{:S(2)}, u32[]{:S(2)}) %collective-permute-start.4) | collective-permute-done | bytes 262176 | tf_op jit(solution)/shard_map/ppermute | solution.py:44
  36.6 3.7 %collective-permute-start.5 = (bf16[32,4096]{1,0:T(8,128)(2,1)S(1)}, bf16[32,4096]{1,0:T(8,128)(2,1)S(1)}, u32[]{:S(2)}, u32[]{:S(2)}) collective-permute-start(bf16[32,4096]{1,0:T(8,128)(2,1)S(1)} %collective-permute-done.4.refs_2_), channel_id=1, source_target_pairs={{0,7},{1,0},{2,1},{3,2},{4,3},{5,4},{6,5},{7,6},{8,15},{9,8},{10,9... | collective-permute-start | bytes 786440 | tf_op jit(solution)/shard_map/ppermute | solution.py:44
  40.3 0.8 convert_reduce_fusion
  41.3 3.8 %collective-permute-done.5.refs_3_ = bf16[32,4096]{1,0:T(8,128)(2,1)S(1)} collective-permute-done((bf16[32,4096]{1,0:T(8,128)(2,1)S(1)}, bf16[32,4096]{1,0:T(8,128)(2,1)S(1)}, u32[]{:S(2)}, u32[]{:S(2)}) %collective-permute-start.5) | collective-permute-done | bytes 262176 | tf_op jit(solution)/shard_map/ppermute | solution.py:44
  45.1 3.8 %collective-permute-start.9 = (bf16[16,4096]{1,0:T(8,128)(2,1)S(1)}, bf16[16,4096]{1,0:T(8,128)(2,1)S(1)}, u32[]{:S(2)}, u32[]{:S(2)}) collective-permute-start(bf16[16,4096]{1,0:T(8,128)(2,1)S(1)} %slice.25), channel_id=1, source_target_pairs={{0,7},{1,0},{2,1},{3,2},{4,3},{5,4},{6,5},{7,6},{8,15},{9,8},{10,9... | collective-permute-start | bytes 393224 | tf_op jit(solution)/shard_map/ppermute | solution.py:44
  49.8 0.9 select_n.61.refs_13_.bias_ref
  50.7 0.8 pad_maximum_fusion.1
  51.5 4.0 %collective-permute-done.8 = bf16[16,4096]{1,0:T(8,128)(2,1)} collective-permute-done((bf16[16,4096]{1,0:T(8,128)(2,1)S(1)}, bf16[16,4096]{1,0:T(8,128)(2,1)}, u32[]{:S(2)}, u32[]{:S(2)}) %collective-permute-start.8) | collective-permute-done | bytes 131104 | tf_op jit(solution)/shard_map/ppermute | solution.py:44
  55.5 1.6 %pad_maximum_fusion.refs_4_ = bf16[32,4096]{1,0:T(8,128)(2,1)} fusion(bf16[16,4096]{1,0:T(8,128)(2,1)S(1)} %collective-permute-done.9, bf16[16,4096]{1,0:T(8,128)(2,1)} %collective-permute-done.8), kind=kLoop, calls=%fused_computation.5 | loop fusion | flops 524288 | bytes 524288 | tf_op jit(solution)/shard_map/concatenate | solution.py:411
  57.1 7.5 %project.1 = (bf16[1536,128]{1,0:T(8,128)(2,1)}, bf16[64,8,256]{2,1,0:T(8,128)(2,1)}) custom-call(s32[1]{0:T(128)} %bitcast.6.z_ref, s32[32]{0:T(128)} %fusion.4.slot_ref, bf16[32,4096]{1,0:T(8,128)(2,1)} %copy-done.6, bf16[32,4096]{1,0:T(8,128)(2,1)} %copy-done.11, bf16[32,4096]{1,0:T(8,128)(2,1)} %copy-done.13, bf16[32,4096]{1,0:T(8,128)(2,1)} %copy-done.9, ...), custom_call_target="tpu_custom_call" | custom-call | flops 1610612736 | bytes 9000000 | tf_op jit(solution)/shard_map/project/pallas_call | solution.py:176
  64.6 6.6 %all-to-all-start = ((bf16[64,8,256]{2,1,0:T(8,128)(2,1)}), bf16[64,8,256]{2,1,0:T(8,128)(2,1)S(1)}, u32[]{:S(2)}, u32[]{:S(2)}) async-start(bf16[64,8,256]{2,1,0:T(8,128)(2,1)} %get-tuple-element.35), calls=%async_computation | async-start | bytes 524288 | tf_op jit(solution)/shard_map/all_to_all | solution.py:439
  71.3 1.0 copy-done.2
  72.3 8.2 %attend.4 = (bf16[32,2048]{1,0:T(8,128)(2,1)S(1)}, bf16[32,2048]{1,0:T(8,128)(2,1)S(1)}, bf16[32,4096]{1,0:T(8,128)(2,1)S(1)}, bf16[8192,256]{1,0:T(8,128)(2,1)S(1)}) custom-call(s32[2]{0:T(128)S(1)} %pad_add_fusion.info_ref, bf16[1536,128]{1,0:T(8,128)(2,1)S(1)} %copy-done.2, f32[1,8192]{1,0:T(1,128)S(1)} %copy-done.4, bf16[512,4096]{1,0:T(8,128)(2,1)} %refs_0_.8, ...), custom_call_target="tpu_custom_call" | custom-call | flops 2214592512 | bytes 9000000 | tf_op jit(solution)/shard_map/attend/pallas_call | solution.py:307
  80.6 3.2 %collective-permute-start.12 = (bf16[32,2048]{1,0:T(8,128)(2,1)S(1)}, bf16[32,2048]{1,0:T(8,128)(2,1)S(1)}, u32[]{:S(2)}, u32[]{:S(2)}) collective-permute-start(bf16[32,2048]{1,0:T(8,128)(2,1)S(1)} %get-tuple-element.45), channel_id=1, source_target_pairs={{0,7},{1,0},{2,1},{3,2},{4,3},{5,4},{6,5},{7,6},{8,15},{9,8},{10,9... | collective-permute-start | bytes 393224 | tf_op jit(solution)/shard_map/ppermute | solution.py:44
  83.8 5.4 %attend.7 = (bf16[32,4096]{1,0:T(8,128)(2,1)S(1)}, bf16[32,4096]{1,0:T(8,128)(2,1)S(1)}) custom-call(s32[2]{0:T(128)S(1)} %pad_add_fusion.info_ref, bf16[1536,128]{1,0:T(8,128)(2,1)S(1)} %copy-done.2, f32[1,8192]{1,0:T(1,128)S(1)} %copy-done.4, bf16[512,4096]{1,0:T(8,128)(2,1)S(1)} %copy-done, bf16[8192,256]{1,0:T(8,128)(2,1)S(1)} %get-tuple-element.41.refs_1_), custom_call_target="tpu_custom_call" | custom-call | flops 2214592512 | bytes 9000000 | tf_op jit(solution)/shard_map/attend/pallas_call | solution.py:307
  89.4 3.2 %collective-permute-start.14 = (bf16[32,4096]{1,0:T(8,128)(2,1)S(1)}, bf16[32,4096]{1,0:T(8,128)(2,1)S(1)}, u32[]{:S(2)}, u32[]{:S(2)}) collective-permute-start(bf16[32,4096]{1,0:T(8,128)(2,1)S(1)} %get-tuple-element.47), channel_id=1, source_target_pairs={{0,7},{1,0},{2,1},{3,2},{4,3},{5,4},{6,5},{7,6},{8,15},{9,8},{10,9... | collective-permute-start | bytes 786440 | tf_op jit(solution)/shard_map/ppermute | solution.py:44
  92.6 8.2 %attend.5 = (bf16[32,4096]{1,0:T(8,128)(2,1)S(1)}, bf16[32,4096]{1,0:T(8,128)(2,1)S(1)}, bf16[8192,256]{1,0:T(8,128)(2,1)S(1)}) custom-call(s32[2]{0:T(128)S(1)} %pad_add_fusion.info_ref, bf16[1536,128]{1,0:T(8,128)(2,1)S(1)} %copy-done.3, f32[1,8192]{1,0:T(1,128)S(1)} %copy-done.4, bf16[512,4096]{1,0:T(8,128)(2,1)} %refs_0_.8, bf16[16384,256]{1,0:T(8,128)(2,1)} %bitcast.21, ...), custom_call_target="tpu_custom_call" | custom-call | flops 2214592512 | bytes 9000000 | tf_op jit(solution)/shard_map/attend/pallas_call | solution.py:307
  101.1 3.2 %collective-permute-start.16 = (bf16[32,4096]{1,0:T(8,128)(2,1)S(1)}, bf16[32,4096]{1,0:T(8,128)(2,1)S(1)}, u32[]{:S(2)}, u32[]{:S(2)}) collective-permute-start(bf16[32,4096]{1,0:T(8,128)(2,1)S(1)} %get-tuple-element.49), channel_id=1, source_target_pairs={{0,7},{1,0},{2,1},{3,2},{4,3},{5,4},{6,5},{7,6},{8,15},{9,8},{10,9... | collective-permute-start | bytes 786440 | tf_op jit(solution)/shard_map/ppermute | solution.py:44
  104.3 6.4 %attend.6 = (bf16[32,4096]{1,0:T(8,128)(2,1)S(1)}, bf16[32,4096]{1,0:T(8,128)(2,1)S(1)}) custom-call(s32[2]{0:T(128)S(1)} %pad_add_fusion.info_ref, bf16[1536,128]{1,0:T(8,128)(2,1)S(1)} %copy-done.3, f32[1,8192]{1,0:T(1,128)S(1)} %copy-done.4, bf16[512,4096]{1,0:T(8,128)(2,1)S(1)} %copy-done.1, bf16[8192,256]{1,0:T(8,128)(2,1)S(1)} %get-tuple-element.36.refs_1_), custom_call_target="tpu_custom_call" | custom-call | flops 2214592512 | bytes 9000000 | tf_op jit(solution)/shard_map/attend/pallas_call | solution.py:307
  111.0 3.2 %collective-permute-start.18 = (bf16[32,4096]{1,0:T(8,128)(2,1)S(1)}, bf16[32,4096]{1,0:T(8,128)(2,1)S(1)}, u32[]{:S(2)}, u32[]{:S(2)}) collective-permute-start(bf16[32,4096]{1,0:T(8,128)(2,1)S(1)} %get-tuple-element.51), channel_id=1, source_target_pairs={{0,7},{1,0},{2,1},{3,2},{4,3},{5,4},{6,5},{7,6},{8,15},{9,8},{10,9... | collective-permute-start | bytes 786440 | tf_op jit(solution)/shard_map/ppermute | solution.py:44
  114.3 1.2 %pick_pages.1 = bf16[32,8,256]{2,1,0:T(8,128)(2,1)} custom-call(s32[32]{0:T(128)S(1)} %select_reduce_fusion.1.source_ref, bf16[64,8,256]{2,1,0:T(8,128)(2,1)S(1)} %all-to-all-done.refs_3_.pages_ref), custom_call_target="tpu_custom_call" | custom-call | bytes 400000 | tf_op jit(solution)/shard_map/pick_pages/pallas_call | solution.py:362
  115.5 3.5 %collective-permute-done.17.from_left_ref = bf16[32,4096]{1,0:T(8,128)(2,1)S(1)} collective-permute-done((bf16[32,4096]{1,0:T(8,128)(2,1)S(1)}, bf16[32,4096]{1,0:T(8,128)(2,1)S(1)}, u32[]{:S(2)}, u32[]{:S(2)}) %collective-permute-start.17) | collective-permute-done | bytes 262176 | tf_op jit(solution)/shard_map/ppermute | solution.py:44
  119.0 0.8 add_rows.1
  (77 shorter events, 4.4 us)
Async XLA Ops:
  1.7 9.2 %collective-permute-start = (bf16[32,4096]{1,0:T(8,128)(2,1)S(1)}, bf16[32,4096]{1,0:T(8,128)(2,1)S(1)}, u32[]{:S(2)}, u32[]{:S(2)}) collective-permute-start(bf16[32,4096]{1,0:T(8,128)(2,1)S(1)} %get-tuple-element.52.refs_0_), channel_id=1, source_target_pairs={{0,8},{8,16},{16,24},{24,32},{32,40},{40,48},{48,56},{56,64},{64,7... | collective-permute-start | bytes 786440 | tf_op jit(solution)/shard_map/ppermute | solution.py:44
  2.6 8.3 %collective-permute-start.1 = (s32[1024]{0:T(1024)S(1)}, s32[1024]{0:T(1024)S(1)}, u32[]{:S(2)}, u32[]{:S(2)}) collective-permute-start(s32[1024]{0:T(1024)S(1)} %bitcast.22), channel_id=1, source_target_pairs={{0,8},{8,16},{16,24},{24,32},{32,40},{40,48},{48,56},{56,64},{64,7... | collective-permute-start | bytes 12296 | tf_op jit(solution)/shard_map/ppermute | solution.py:44
  9.0 16.8 %copy-start.7 = (s32[32,32]{1,0:T(8,128)S(1)}, s32[32,32]{1,0:T(8,128)}, u32[]{:S(2)}) copy-start(s32[32,32]{1,0:T(8,128)} %refs_1_.1) | copy-start | bytes 12292
  11.2 45.9 %copy-start.6 = (bf16[32,4096]{1,0:T(8,128)(2,1)}, bf16[32,4096]{1,0:T(8,128)(2,1)S(1)}, u32[]{:S(2)}) copy-start(bf16[32,4096]{1,0:T(8,128)(2,1)S(1)} %get-tuple-element.28.refs_0_) | copy-start | bytes 786436
  11.2 60.0 %collective-permute-start.10 = (bf16[1024,8,256]{2,1,0:T(8,128)(2,1)}, bf16[1024,8,256]{2,1,0:T(8,128)(2,1)}, u32[]{:S(2)}, u32[]{:S(2)}) collective-permute-start(bf16[1024,8,256]{2,1,0:T(8,128)(2,1)} %get-tuple-element.33), channel_id=1, source_target_pairs={{0,8},{8,16},{16,24},{24,32},{32,40},{40,48},{48,56},{56,64},{64,7... | collective-permute-start | bytes 12582920 | tf_op jit(solution)/shard_map/ppermute | solution.py:44
  11.3 16.6 %collective-permute-start.3 = (bf16[32,4096]{1,0:T(8,128)(2,1)S(1)}, bf16[32,4096]{1,0:T(8,128)(2,1)S(1)}, u32[]{:S(2)}, u32[]{:S(2)}) collective-permute-start(bf16[32,4096]{1,0:T(8,128)(2,1)S(1)} %get-tuple-element.28.refs_0_), channel_id=1, source_target_pairs={{0,7},{1,0},{2,1},{3,2},{4,3},{5,4},{6,5},{7,6},{8,15},{9,8},{10,9... | collective-permute-start | bytes 786440 | tf_op jit(solution)/shard_map/ppermute | solution.py:44
  15.5 10.3 %collective-permute-start.2 = (bf16[32,4096]{1,0:T(8,128)(2,1)S(1)}, bf16[32,4096]{1,0:T(8,128)(2,1)S(1)}, u32[]{:S(2)}, u32[]{:S(2)}) collective-permute-start(bf16[32,4096]{1,0:T(8,128)(2,1)S(1)} %get-tuple-element.28.refs_0_), channel_id=1, source_target_pairs={{0,1},{1,2},{2,3},{3,4},{4,5},{5,6},{6,7},{7,0},{8,9},{9,10},{10,1... | collective-permute-start | bytes 786440 | tf_op jit(solution)/shard_map/ppermute | solution.py:44
  25.8 31.3 %copy-start.5 = (bf16[32,4096]{1,0:T(8,128)(2,1)}, bf16[32,4096]{1,0:T(8,128)(2,1)S(1)}, u32[]{:S(2)}) copy-start(bf16[32,4096]{1,0:T(8,128)(2,1)S(1)} %collective-permute-done.2.refs_3_.refs_7_) | copy-start | bytes 786436
  27.8 12.6 %collective-permute-start.6 = (bf16[32,4096]{1,0:T(8,128)(2,1)S(1)}, bf16[32,4096]{1,0:T(8,128)(2,1)S(1)}, u32[]{:S(2)}, u32[]{:S(2)}) collective-permute-start(bf16[32,4096]{1,0:T(8,128)(2,1)S(1)} %collective-permute-done.2.refs_3_.refs_7_), channel_id=1, source_target_pairs={{0,1},{1,2},{2,3},{3,4},{4,5},{5,6},{6,7},{7,0},{8,9},{9,10},{10,1... | collective-permute-start | bytes 786440 | tf_op jit(solution)/shard_map/ppermute | solution.py:44
  27.9 29.2 %copy-start.11 = (bf16[32,4096]{1,0:T(8,128)(2,1)}, bf16[32,4096]{1,0:T(8,128)(2,1)S(1)}, u32[]{:S(2)}) copy-start(bf16[32,4096]{1,0:T(8,128)(2,1)S(1)} %collective-permute-done.3.refs_1_) | copy-start | bytes 786436
  27.9 8.8 %collective-permute-start.4 = (bf16[32,4096]{1,0:T(8,128)(2,1)S(1)}, bf16[32,4096]{1,0:T(8,128)(2,1)S(1)}, u32[]{:S(2)}, u32[]{:S(2)}) collective-permute-start(bf16[32,4096]{1,0:T(8,128)(2,1)S(1)} %collective-permute-done.3.refs_1_), channel_id=1, source_target_pairs={{0,7},{1,0},{2,1},{3,2},{4,3},{5,4},{6,5},{7,6},{8,15},{9,8},{10,9... | collective-permute-start | bytes 786440 | tf_op jit(solution)/shard_map/ppermute | solution.py:44
  36.6 20.5 %copy-start.13 = (bf16[32,4096]{1,0:T(8,128)(2,1)}, bf16[32,4096]{1,0:T(8,128)(2,1)S(1)}, u32[]{:S(2)}) copy-start(bf16[32,4096]{1,0:T(8,128)(2,1)S(1)} %collective-permute-done.4.refs_2_) | copy-start | bytes 786436
  36.6 8.5 %collective-permute-start.5 = (bf16[32,4096]{1,0:T(8,128)(2,1)S(1)}, bf16[32,4096]{1,0:T(8,128)(2,1)S(1)}, u32[]{:S(2)}, u32[]{:S(2)}) collective-permute-start(bf16[32,4096]{1,0:T(8,128)(2,1)S(1)} %collective-permute-done.4.refs_2_), channel_id=1, source_target_pairs={{0,7},{1,0},{2,1},{3,2},{4,3},{5,4},{6,5},{7,6},{8,15},{9,8},{10,9... | collective-permute-start | bytes 786440 | tf_op jit(solution)/shard_map/ppermute | solution.py:44
  40.3 16.8 %copy-start.12 = (bf16[32,4096]{1,0:T(8,128)(2,1)}, bf16[32,4096]{1,0:T(8,128)(2,1)S(1)}, u32[]{:S(2)}) copy-start(bf16[32,4096]{1,0:T(8,128)(2,1)S(1)} %collective-permute-done.6.refs_6_) | copy-start | bytes 786436
  40.3 8.6 %collective-permute-start.7 = (bf16[32,4096]{1,0:T(8,128)(2,1)S(1)}, bf16[32,4096]{1,0:T(8,128)(2,1)S(1)}, u32[]{:S(2)}, u32[]{:S(2)}) collective-permute-start(bf16[32,4096]{1,0:T(8,128)(2,1)S(1)} %collective-permute-done.6.refs_6_), channel_id=1, source_target_pairs={{0,1},{1,2},{2,3},{3,4},{4,5},{5,6},{6,7},{7,0},{8,9},{9,10},{10,1... | collective-permute-start | bytes 786440 | tf_op jit(solution)/shard_map/ppermute | solution.py:44
  45.1 12.0 %copy-start.9 = (bf16[32,4096]{1,0:T(8,128)(2,1)}, bf16[32,4096]{1,0:T(8,128)(2,1)S(1)}, u32[]{:S(2)}) copy-start(bf16[32,4096]{1,0:T(8,128)(2,1)S(1)} %collective-permute-done.5.refs_3_) | copy-start | bytes 786436
  45.1 6.4 %collective-permute-start.9 = (bf16[16,4096]{1,0:T(8,128)(2,1)S(1)}, bf16[16,4096]{1,0:T(8,128)(2,1)S(1)}, u32[]{:S(2)}, u32[]{:S(2)}) collective-permute-start(bf16[16,4096]{1,0:T(8,128)(2,1)S(1)} %slice.25), channel_id=1, source_target_pairs={{0,7},{1,0},{2,1},{3,2},{4,3},{5,4},{6,5},{7,6},{8,15},{9,8},{10,9... | collective-permute-start | bytes 393224 | tf_op jit(solution)/shard_map/ppermute | solution.py:44
  48.9 8.2 %copy-start.10 = (bf16[32,4096]{1,0:T(8,128)(2,1)}, bf16[32,4096]{1,0:T(8,128)(2,1)S(1)}, u32[]{:S(2)}) copy-start(bf16[32,4096]{1,0:T(8,128)(2,1)S(1)} %collective-permute-done.7.refs_5_) | copy-start | bytes 786436
  48.9 6.5 %collective-permute-start.8 = (bf16[16,4096]{1,0:T(8,128)(2,1)S(1)}, bf16[16,4096]{1,0:T(8,128)(2,1)}, u32[]{:S(2)}, u32[]{:S(2)}) collective-permute-start(bf16[16,4096]{1,0:T(8,128)(2,1)S(1)} %slice.24), channel_id=1, source_target_pairs={{0,1},{1,2},{2,3},{3,4},{4,5},{5,6},{6,7},{7,0},{8,9},{9,10},{10,1... | collective-permute-start | bytes 393224 | tf_op jit(solution)/shard_map/ppermute | solution.py:44
  57.1 14.1 %copy-start.4 = (f32[1,8192]{1,0:T(1,128)S(1)}, f32[1,8192]{1,0:T(1,128)}, u32[]{:S(2)}) copy-start(f32[1,8192]{1,0:T(1,128)} %select_n.61.refs_13_.bias_ref) | copy-start | bytes 98308
  64.6 28.0 %all-to-all-start = ((bf16[64,8,256]{2,1,0:T(8,128)(2,1)}), bf16[64,8,256]{2,1,0:T(8,128)(2,1)S(1)}, u32[]{:S(2)}, u32[]{:S(2)}) async-start(bf16[64,8,256]{2,1,0:T(8,128)(2,1)} %get-tuple-element.35), calls=%async_computation | async-start | bytes 524288 | tf_op jit(solution)/shard_map/all_to_all | solution.py:439
  72.2 11.5 %copy-start = (bf16[512,4096]{1,0:T(8,128)(2,1)S(1)}, bf16[512,4096]{1,0:T(8,128)(2,1)}, u32[]{:S(2)}) copy-start(bf16[512,4096]{1,0:T(8,128)(2,1)} %refs_0_.8) | copy-start | bytes 12582916
  80.5 8.8 %collective-permute-start.11 = (bf16[32,2048]{1,0:T(8,128)(2,1)S(1)}, bf16[32,2048]{1,0:T(8,128)(2,1)S(1)}, u32[]{:S(2)}, u32[]{:S(2)}) collective-permute-start(bf16[32,2048]{1,0:T(8,128)(2,1)S(1)} %get-tuple-element.44), channel_id=1, source_target_pairs={{0,1},{1,2},{2,3},{3,4},{4,5},{5,6},{6,7},{7,0},{8,9},{9,10},{10,1... | collective-permute-start | bytes 393224 | tf_op jit(solution)/shard_map/ppermute | solution.py:44
  80.6 8.7 %collective-permute-start.12 = (bf16[32,2048]{1,0:T(8,128)(2,1)S(1)}, bf16[32,2048]{1,0:T(8,128)(2,1)S(1)}, u32[]{:S(2)}, u32[]{:S(2)}) collective-permute-start(bf16[32,2048]{1,0:T(8,128)(2,1)S(1)} %get-tuple-element.45), channel_id=1, source_target_pairs={{0,7},{1,0},{2,1},{3,2},{4,3},{5,4},{6,5},{7,6},{8,15},{9,8},{10,9... | collective-permute-start | bytes 393224 | tf_op jit(solution)/shard_map/ppermute | solution.py:44
  83.8 8.9 %copy-start.3 = (bf16[1536,128]{1,0:T(8,128)(2,1)S(1)}, bf16[1536,128]{1,0:T(8,128)(2,1)}, u32[]{:S(2)}) copy-start(bf16[1536,128]{1,0:T(8,128)(2,1)} %get-tuple-element.32.q_ref) | copy-start | bytes 1179652
  89.3 11.5 %collective-permute-start.13 = (bf16[32,4096]{1,0:T(8,128)(2,1)S(1)}, bf16[32,4096]{1,0:T(8,128)(2,1)S(1)}, u32[]{:S(2)}, u32[]{:S(2)}) collective-permute-start(bf16[32,4096]{1,0:T(8,128)(2,1)S(1)} %get-tuple-element.46), channel_id=1, source_target_pairs={{0,1},{1,2},{2,3},{3,4},{4,5},{5,6},{6,7},{7,0},{8,9},{9,10},{10,1... | collective-permute-start | bytes 786440 | tf_op jit(solution)/shard_map/ppermute | solution.py:44
  89.4 11.5 %collective-permute-start.14 = (bf16[32,4096]{1,0:T(8,128)(2,1)S(1)}, bf16[32,4096]{1,0:T(8,128)(2,1)S(1)}, u32[]{:S(2)}, u32[]{:S(2)}) collective-permute-start(bf16[32,4096]{1,0:T(8,128)(2,1)S(1)} %get-tuple-element.47), channel_id=1, source_target_pairs={{0,7},{1,0},{2,1},{3,2},{4,3},{5,4},{6,5},{7,6},{8,15},{9,8},{10,9... | collective-permute-start | bytes 786440 | tf_op jit(solution)/shard_map/ppermute | solution.py:44
  92.6 11.7 %copy-start.1 = (bf16[512,4096]{1,0:T(8,128)(2,1)S(1)}, bf16[512,4096]{1,0:T(8,128)(2,1)}, u32[]{:S(2)}) copy-start(bf16[512,4096]{1,0:T(8,128)(2,1)} %refs_0_.8) | copy-start | bytes 12582916
  101.0 9.7 %collective-permute-start.15 = (bf16[32,4096]{1,0:T(8,128)(2,1)S(1)}, bf16[32,4096]{1,0:T(8,128)(2,1)S(1)}, u32[]{:S(2)}, u32[]{:S(2)}) collective-permute-start(bf16[32,4096]{1,0:T(8,128)(2,1)S(1)} %get-tuple-element.48), channel_id=1, source_target_pairs={{0,1},{1,2},{2,3},{3,4},{4,5},{5,6},{6,7},{7,0},{8,9},{9,10},{10,1... | collective-permute-start | bytes 786440 | tf_op jit(solution)/shard_map/ppermute | solution.py:44
  101.1 9.6 %collective-permute-start.16 = (bf16[32,4096]{1,0:T(8,128)(2,1)S(1)}, bf16[32,4096]{1,0:T(8,128)(2,1)S(1)}, u32[]{:S(2)}, u32[]{:S(2)}) collective-permute-start(bf16[32,4096]{1,0:T(8,128)(2,1)S(1)} %get-tuple-element.49), channel_id=1, source_target_pairs={{0,7},{1,0},{2,1},{3,2},{4,3},{5,4},{6,5},{7,6},{8,15},{9,8},{10,9... | collective-permute-start | bytes 786440 | tf_op jit(solution)/shard_map/ppermute | solution.py:44
  110.9 8.1 %collective-permute-start.17 = (bf16[32,4096]{1,0:T(8,128)(2,1)S(1)}, bf16[32,4096]{1,0:T(8,128)(2,1)S(1)}, u32[]{:S(2)}, u32[]{:S(2)}) collective-permute-start(bf16[32,4096]{1,0:T(8,128)(2,1)S(1)} %get-tuple-element.50), channel_id=1, source_target_pairs={{0,1},{1,2},{2,3},{3,4},{4,5},{5,6},{6,7},{7,0},{8,9},{9,10},{10,1... | collective-permute-start | bytes 786440 | tf_op jit(solution)/shard_map/ppermute | solution.py:44
  111.0 8.0 %collective-permute-start.18 = (bf16[32,4096]{1,0:T(8,128)(2,1)S(1)}, bf16[32,4096]{1,0:T(8,128)(2,1)S(1)}, u32[]{:S(2)}, u32[]{:S(2)}) collective-permute-start(bf16[32,4096]{1,0:T(8,128)(2,1)S(1)} %get-tuple-element.51), channel_id=1, source_target_pairs={{0,7},{1,0},{2,1},{3,2},{4,3},{5,4},{6,5},{7,6},{8,15},{9,8},{10,9... | collective-permute-start | bytes 786440 | tf_op jit(solution)/shard_map/ppermute | solution.py:44
  (4 other events, 13.9 us)
